TPU v7x, 512 devices: a whole 4x4x16 slice. The times are simulated.
512 devices in a mesh: depth: 8 (over z_lo), row: 8 (over y, core), col: 8 (over z_hi, x).
Axes of the slice: x: 4, y: 4, z: 16 (z_hi: 2, z_lo: 8; z = z_hi * 8 + z_lo), core: 2. Of those that a mesh axis runs over, the one named last changes fastest.
Arguments:
- tokens: bfloat16 [256, 12288], P(('depth', 'row'), 'col'), may hold values from -6 to 6
- w_up: bfloat16 [24576, 12288], P(('depth', 'row'), 'col'), may hold values from -0.0546875 to 0.0546875
- w_down: bfloat16 [24576, 12288], P(('depth', 'row'), 'col'), may hold values from -0.0390625 to 0.0390625
- grad_out: bfloat16 [256, 12288], P(('depth', 'row'), 'col'), may hold values from -6 to 6
Outputs:
- out: bfloat16 [256, 12288], P(('depth', 'row'), 'col')
- grad_in: bfloat16 [256, 12288], P(('depth', 'row'), 'col')
- grad_w_up: bfloat16 [24576, 12288], P(('depth', 'row'), 'col')
- grad_w_down: bfloat16 [24576, 12288], P(('depth', 'row'), 'col')
All inputs are finite; a program needn't handle non-finite values.
Results may differ from a plain program's by a relative error of at most 0.024.
Values may be sent and summed in bfloat16 or wider, within the bound.
A program may use at most 64 MiB of HBM per device.

v0:
```python
import math

import jax
import jax.numpy as jnp
from jax import lax
from jax.sharding import PartitionSpec as P

coeff = 0.7978845608028654


def gelu_value(value):
    inner = jnp.tanh(coeff * (value + 0.044715 * value * value * value))
    return 0.5 * value * (1.0 + inner)


def gelu_slope(value):
    inner = jnp.tanh(coeff * (value + 0.044715 * value * value * value))
    return 0.5 * (1.0 + inner) + 0.5 * value * (1.0 - inner * inner) * coeff * (
        1.0 + 3.0 * 0.044715 * value * value
    )


def along_rows(left, right):
    return lax.dot_general(
        left, right, (((1,), (1,)), ((), ())), preferred_element_type=jnp.float32
    )


def over_tokens(left, right):
    return lax.dot_general(
        left, right, (((0,), (0,)), ((), ())), preferred_element_type=jnp.float32
    )


def spread_sum(hidden_rows, weight):
    summed = lax.psum_scatter(
        jnp.dot(hidden_rows, weight, preferred_element_type=jnp.float32),
        ("depth", "row"),
        scatter_dimension=0,
        tiled=True,
    )
    return summed.astype(jnp.bfloat16)


def local(tokens, w_up, w_down, grad_out):
    tok_all, grad_all = (
        lax.all_gather(tokens, ("depth", "row"), axis=0, tiled=True),
        lax.all_gather(grad_out, ("depth", "row"), axis=0, tiled=True),
    )
    scale = 1.0 / math.sqrt(tok_all.shape[0])
    pre = lax.psum(along_rows(tok_all, w_up).astype(jnp.bfloat16), "col").astype(jnp.float32)
    act = gelu_value(pre).astype(jnp.bfloat16)
    out = spread_sum(act, w_down)
    grad_act = lax.psum(along_rows(grad_all, w_down).astype(jnp.bfloat16), "col").astype(
        jnp.float32
    )
    grad_pre = (grad_act * gelu_slope(pre)).astype(jnp.bfloat16)
    grad_in = spread_sum(grad_pre, w_up)
    grad_w_up = (over_tokens(grad_pre, tok_all) * scale).astype(jnp.bfloat16)
    grad_w_down = (over_tokens(act, grad_all) * scale).astype(jnp.bfloat16)
    return (out, grad_in, grad_w_up, grad_w_down)


def solution(mesh):
    in_specs = (
        P(("depth", "row"), "col"),
        P(("depth", "row"), "col"),
        P(("depth", "row"), "col"),
        P(("depth", "row"), "col"),
    )
    out_specs = (
        P(("depth", "row"), "col"),
        P(("depth", "row"), "col"),
        P(("depth", "row"), "col"),
        P(("depth", "row"), "col"),
    )
    return jax.shard_map(local, mesh=mesh, in_specs=in_specs, out_specs=out_specs, check_vma=False)
```

profile of v0, /device:TPU:1, one launch (start us, length us, event | category | flops | bytes accessed | tf_op | source)
XLA Modules:
  0.0 859.4 jit_solution(12230198265651077648)
XLA Ops:
  7.2 0.0 copy-start
  7.2 0.0 all-reduce.7.cloned.1.call-start
  7.2 0.0 copy-start.4
  7.2 129.6 %all-gather.1 = bf16[64,4,1536]{2,1,0:T(4,128)(2,1)S(1)} all-gather(bf16[1,4,1536]{2,1,0:T(4,128)(2,1)} %bitcast.11), channel_id=1, replica_groups=mesh['depth'=8,'row'=8,'col'=8] {'depth','row'}, dimensions={0}, use_global_device_ids=true | all-gather | bytes 798720 | tf_op jit(solution)/shard_map/all_gather | solution.py:48
  136.8 0.2 reshape.11
  137.0 0.0 copy-done.4
  137.0 114.5 %all-gather = bf16[64,4,1536]{2,1,0:T(4,128)(2,1)S(1)} all-gather(bf16[1,4,1536]{2,1,0:T(4,128)(2,1)S(1)} %bitcast.12), channel_id=1, replica_groups=mesh['depth'=8,'row'=8,'col'=8] {'depth','row'}, dimensions={0}, use_global_device_ids=true | all-gather | bytes 798720 | tf_op jit(solution)/shard_map/all_gather | solution.py:47
  251.6 0.2 reshape.9
  251.8 0.0 copy-done
  251.8 0.0 copy-start.1
  251.8 0.0 copy-start.5
  251.8 1.3 convolution_convert_fusion
  253.1 0.3 copy-done.5
  253.4 1.3 convolution_convert_fusion.1
  254.7 0.0 copy-done.1
  254.7 0.0 all-reduce.7.cloned.1.call-update
  254.7 1.3 dynamic-slice
  256.6 141.3 %all-reduce.7.cloned.1.call-done = (bf16[256,384]{1,0:T(8,128)(2,1)}, bf16[256,384]{1,0:T(8,128)(2,1)}) async-done(((bf16[256,384]{1,0:T(8,128)(2,1)}, bf16[256,384]{1,0:T(8,128)(2,1)}), (bf16[256,384]{1,0:T(8,128)(2,1)}, bf16[256,384]{1,0:T(8,128)(2,1)})) %all-reduce.7.cloned.1.call-update) | async-done | bytes 393232 | tf_op jit(solution)/shard_map/psum | solution.py:51
  397.9 0.0 copy-start.3
  397.9 0.0 copy-start.6
  397.9 0.0 copy-start.7
  397.9 1.6 fusion.14
  399.5 0.0 copy-done.3
  399.6 0.0 copy-done.6
  399.6 0.0 copy-done.7
  399.6 0.0 copy-start.2
  399.6 1.9 fusion.17
  401.5 0.0 copy-done.2
  401.5 1.7 fusion
  403.2 1.6 fusion.1
  404.8 446.4 %all-reduce.8 = (bf16[256,1536]{1,0:T(8,128)(2,1)S(1)}, bf16[256,1536]{1,0:T(8,128)(2,1)}) all-reduce(f32[256,1536]{1,0:T(8,128)S(1)} %fusion.14, f32[256,1536]{1,0:T(8,128)} %fusion.17), channel_id=2, replica_groups=mesh['depth'=8,'row'=8,'col'=8] {'depth','row'}, use_global_device_ids=true, to_apply=%region_1.0.clone | all-reduce | flops 786432 | bytes 4718592
  851.2 1.4 dynamic-slice_convert_fusion
Async XLA Ops:
  7.2 244.6 %copy-start = (bf16[384,1536]{1,0:T(8,128)(2,1)S(1)}, bf16[384,1536]{1,0:T(8,128)(2,1)}, u32[]{:S(2)}) copy-start(bf16[384,1536]{1,0:T(8,128)(2,1)} %param.6) | copy-start | bytes 3538948
  7.2 390.7 %all-reduce.7.cloned.1.call-start = ((), (), s32[]{:S(2)}) async-start(), calls=%async_computation | async-start | bytes 786432 | tf_op jit(solution)/shard_map/psum | solution.py:51
  7.2 129.8 %copy-start.4 = (bf16[4,1536]{1,0:T(4,128)(2,1)S(1)}, bf16[4,1536]{1,0:T(4,128)(2,1)}, u32[]{:S(2)}) copy-start(bf16[4,1536]{1,0:T(4,128)(2,1)} %param.4) | copy-start | bytes 36868
  251.8 2.9 copy-start.1
  251.8 1.6 copy-start.5
  397.9 1.6 copy-start.3
  397.9 1.7 copy-start.6
  397.9 1.7 copy-start.7
  399.6 1.9 copy-start.2
Sparse Core Ops, SparseCore 0:
  254.8 143.0 all-reduce.6
where the time goes:
time: 868 us; the launch traced here: 859 us
  blocking collectives  691 us (80%)
  waiting for transfers between devices  141 us (16%)
  between operations  14.8 us (2%)
  matrix products  9.34 us (1%)
    unnamed x1, blocking collectives  446 us
    psum x1, waiting for transfers between devices, local(): lax.psum(along_rows(tok_all, w_up).astype(jnp.bfloat16), 'col')  141 us
    all_gather x1, blocking collectives, local(): lax.all_gather(grad_out, ('depth', 'row'), axis=0, tiled=True)  130 us
    all_gather x1, blocking collectives, local(): lax.all_gather(tokens, ('depth', 'row'), axis=0, tiled=True)  115 us
  transfers between devices with their start and end apart: 1, of which 1 were waited for; matrix products, arithmetic and copies ran while one was open for 0% of the time, Pallas kernels for 0%

commit v1 on v0

v1 whole, which is shorter than its diff:
```python
import functools
import math

import jax
import jax.numpy as jnp
from jax import lax
from jax.experimental import pallas as pl
from jax.experimental.pallas import tpu as pltpu
from jax.sharding import PartitionSpec as P

MESH = pl.DeviceIdType.MESH
NX, NY, NZ = 4, 4, 8
F32, BF16 = jnp.float32, jnp.bfloat16
coeff = 0.7978845608028654


def gelu_value(value):
    inner = jnp.tanh(coeff * (value + 0.044715 * value * value * value))
    return 0.5 * value * (1.0 + inner)


def gelu_slope(value):
    inner = jnp.tanh(coeff * (value + 0.044715 * value * value * value))
    return 0.5 * (1.0 + inner) + 0.5 * value * (1.0 - inner * inner) * coeff * (
        1.0 + 3.0 * 0.044715 * value * value
    )


def along_rows(left, right):
    return lax.dot_general(left, right, (((1,), (1,)), ((), ())), preferred_element_type=F32)


def over_tokens(left, right):
    return lax.dot_general(left, right, (((0,), (0,)), ((), ())), preferred_element_type=F32)


def kernel(
    scale,
    tok_ref, w_up_ref, w_down_ref, grad_ref,
    out_ref, gin_ref, gwu_ref, gwd_ref,
    weights, wouts, pieces, full, part, xin, far_out, far_in, hidden,
    core_out, core_in, y_out, y_in, z_out, z_in, last_out, last_in,
    w_sem, o_sem, az, ay, ac, xr, fz, xa, rc, ry, rz, rl,
):
    depth, row, col = lax.axis_index("depth"), lax.axis_index("row"), lax.axis_index("col")
    z, y, core, x = depth, row // 2, row % 2, col % NX

    def at(z=depth, y=y, core=core, col=col):
        return {"depth": z, "row": y * 2 + core, "col": col}

    z_peers = [(z + k) % NZ for k in (4, 3, 5, 2, 6, 1, 7)]
    y_peers = [(y + k) % NY for k in (2, 1, 3)]
    x_peers = [(x + k) % NX for k in (2, 1, 3)]
    along_z = [at(z=p) for p in z_peers]
    along_y = [at(y=p) for p in y_peers]
    along_x = [at(col=col - x + p) for p in x_peers]
    other = at(core=1 - core)
    far = at(col=(col + NX) % (2 * NX))

    def copy(src, dst, sems, send_at, recv_at, to):
        return pltpu.make_async_remote_copy(
            src_ref=src, dst_ref=dst, send_sem=sems.at[(0, *send_at)], recv_sem=sems.at[(1, *recv_at)],
            device_id=to, device_id_type=MESH,
        )

    started = []

    def send(*args):
        c = copy(*args)
        c.start()
        started.append(c)

    def arrive(dst, sems, recv_at):
        copy(dst, dst, sems, recv_at, recv_at, other).wait_recv()

    loads = [
        pltpu.make_async_copy(ref, weights.at[i], w_sem.at[i]) for i, ref in enumerate((w_up_ref, w_down_ref))
    ]
    for c in loads:
        c.start()

    barrier = pltpu.get_barrier_semaphore()
    everyone = [*along_z, *along_y, *along_x, other, far]
    for d in everyone:
        pl.semaphore_signal(barrier, inc=1, device_id=d, device_id_type=MESH)

    for s, ref in enumerate((tok_ref, grad_ref)):
        v = ref[...].astype(F32)
        folded = jnp.concatenate([v[:, 384 * c : 384 * (c + 1)] for c in range(4)], axis=0)
        pieces[s, y, core, z] = folded.astype(BF16)
    pl.semaphore_wait(barrier, len(everyone))

    for s in range(2):
        mine = pieces.at[s, y, core, z]
        for p, d in zip(z_peers, along_z, strict=True):
            send(mine, mine, az, (s, p), (s, z), d)
    for s in range(2):
        for p in reversed(z_peers):
            arrive(pieces.at[s, y, core, p], az, (s, p))
        mine = pieces.at[s, y, core]
        for p, d in zip(y_peers, along_y, strict=True):
            send(mine, mine, ay, (s, p), (s, y), d)
        send(mine, mine, ac, (s, y), (s, y), other)

    top = lax.broadcasted_iota(jnp.int32, (NZ, 8, 384), 1) < 4

    def gather_rest(s):
        for p in (y_peers[1], y_peers[2], y_peers[0]):
            block = pieces.at[s, p, core]
            arrive(block, ay, (s, p))
            send(block, block, ac, (s, p), (s, p), other)
        for q in range(NY):
            arrive(pieces.at[s, q, 1 - core], ac, (s, q))
        for q in range(NY):
            halves = [pieces[s, q, k].astype(F32).reshape(NZ, 2, 8, 384) for k in range(2)]
            for c in range(4):
                first, second = halves[0][:, c // 2], halves[1][:, c // 2]
                if c % 2 == 0:
                    block = jnp.where(top, first, pltpu.roll(second, 4, 1))
                else:
                    block = jnp.where(top, pltpu.roll(first, 4, 1), second)
                full[s, 64 * q : 64 * (q + 1), 384 * c : 384 * (c + 1)] = block.reshape(64, 384).astype(BF16)

    for s in range(2):
        gather_rest(s)
        loads[s].wait()
        for q in range(NX):
            part[s, q] = along_rows(full[s, 64 * q : 64 * (q + 1), :], weights[s]).astype(BF16)
        for p, d in zip(x_peers, along_x, strict=True):
            send(part.at[s, p], xin.at[s, x], xr, (s, p), (s, x), d)
    for s in range(2):
        total = part[s, x].astype(F32)
        for p in (x_peers[1], x_peers[2], x_peers[0]):
            arrive(xin.at[s, p], xr, (s, p))
            total += xin[s, p].astype(F32)
        far_out[s] = total.astype(BF16)
        send(far_out.at[s], far_in.at[s], fz, (s,), (s,), far)
    sums = []
    for s in range(2):
        arrive(far_in.at[s], fz, (s,))
        sums.append(far_out[s].astype(F32) + far_in[s].astype(F32))
        if s == 0:
            hidden[0, x] = gelu_value(sums[0]).astype(BF16)
        else:
            hidden[1, x] = (sums[1] * gelu_slope(sums[0])).astype(BF16)
        mine = hidden.at[s, x]
        for p, d in zip(x_peers, along_x, strict=True):
            send(mine, mine, xa, (s, p), (s, x), d)

    own = pl.multiple_of(core * 768, 128)
    not_own = pl.multiple_of((1 - core) * 768, 128)
    for s in range(2):
        for p in (x_peers[1], x_peers[2], x_peers[0]):
            arrive(hidden.at[s, p], xa, (s, p))
        w = weights.at[1 - s]
        h = hidden[s].reshape(256, 384)
        core_out[s] = jnp.dot(h, w[:, pl.ds(not_own, 768)], preferred_element_type=F32).astype(BF16)
        send(core_out.at[s], core_in.at[s], rc, (s,), (s,), other)
    for s in range(2):
        h = hidden[s].reshape(256, 384)
        part_out = jnp.dot(h, weights[1 - s, :, pl.ds(own, 768)], preferred_element_type=F32)
        arrive(core_in.at[s], rc, (s,))
        y_out[s] = (part_out + core_in[s].astype(F32)).astype(BF16).reshape(NY, 64, 768)
        for p, d in zip(y_peers, along_y, strict=True):
            send(y_out.at[s, p], y_in.at[s, y], ry, (s, p), (s, y), d)

    stores = []
    for s, ref in ((1, gwd_ref), (0, gwu_ref)):
        h = hidden[1 - s].reshape(256, 384)
        for c in range(4):
            cols = slice(384 * c, 384 * (c + 1))
            wouts[s, :, cols] = (over_tokens(h, full[s, :, cols]) * scale).astype(BF16)
        c = pltpu.make_async_copy(wouts.at[s], ref, o_sem.at[s])
        c.start()
        stores.append(c)

    for s in range(2):
        total = y_out[s, y].astype(F32)
        for p in (y_peers[1], y_peers[2], y_peers[0]):
            arrive(y_in.at[s, p], ry, (s, p))
            total += y_in[s, p].astype(F32)
        rows = total.reshape(NZ, 8, 768)
        z_out[s] = jnp.concatenate([rows[:, :, :384], rows[:, :, 384:]], axis=1).astype(BF16)
        for p, d in zip(z_peers, along_z, strict=True):
            send(z_out.at[s, p], z_in.at[s, z], rz, (s, p), (s, z), d)
    for s in range(2):
        total = z_out[s, z].astype(F32)
        for p in reversed(z_peers):
            arrive(z_in.at[s, p], rz, (s, p))
            total += z_in[s, p].astype(F32)
        last_out[s] = total.astype(BF16)
        send(last_out.at[s], last_in.at[s], rl, (s,), (s,), other)
    for s, ref in ((0, out_ref), (1, gin_ref)):
        arrive(last_in.at[s], rl, (s,))
        mine, theirs = last_out[s].astype(F32), last_in[s].astype(F32)
        left = jnp.where(core == 0, mine, theirs)
        right = jnp.where(core == 0, theirs, mine)
        rows = jnp.concatenate([left[:8], left[8:], right[:8], right[8:]], axis=1)
        ref[...] = jnp.where(core == 0, rows[:4], rows[4:]).astype(BF16)
    for c in started:
        c.wait_send()
    for c in stores:
        c.wait()


def local(tokens, w_up, w_down, grad_out):
    n_tokens = tokens.shape[0] * lax.axis_size("depth") * lax.axis_size("row")
    scale = 1.0 / math.sqrt(n_tokens)
    vmem, hbm = pl.BlockSpec(memory_space=pltpu.VMEM), pl.BlockSpec(memory_space=pl.ANY)
    dma = pltpu.SemaphoreType.DMA
    shape = jax.ShapeDtypeStruct
    return pl.pallas_call(
        functools.partial(kernel, scale),
        name="ffn",
        out_shape=(
            shape((4, 1536), BF16), shape((4, 1536), BF16), shape((384, 1536), BF16), shape((384, 1536), BF16),
        ),
        in_specs=[vmem, hbm, hbm, vmem],
        out_specs=(vmem, vmem, hbm, hbm),
        scratch_shapes=[
            pltpu.VMEM((2, 384, 1536), BF16),
            pltpu.VMEM((2, 384, 1536), BF16),
            pltpu.VMEM((2, NY, 2, NZ, 16, 384), BF16),
            pltpu.VMEM((2, 256, 1536), BF16),
            pltpu.VMEM((2, NX, 64, 384), BF16),
            pltpu.VMEM((2, NX, 64, 384), BF16),
            pltpu.VMEM((2, 64, 384), BF16),
            pltpu.VMEM((2, 64, 384), BF16),
            pltpu.VMEM((2, NX, 64, 384), BF16),
            pltpu.VMEM((2, 256, 768), BF16),
            pltpu.VMEM((2, 256, 768), BF16),
            pltpu.VMEM((2, NY, 64, 768), BF16),
            pltpu.VMEM((2, NY, 64, 768), BF16),
            pltpu.VMEM((2, NZ, 16, 384), BF16),
            pltpu.VMEM((2, NZ, 16, 384), BF16),
            pltpu.VMEM((2, 16, 384), BF16),
            pltpu.VMEM((2, 16, 384), BF16),
            dma((2,)), dma((2,)),
            dma((2, 2, NZ)), dma((2, 2, NY)), dma((2, 2, NY)), dma((2, 2, NX)), dma((2, 2)), dma((2, 2, NX)),
            dma((2, 2)), dma((2, 2, NY)), dma((2, 2, NZ)), dma((2, 2)),
        ],
        compiler_params=pltpu.CompilerParams(
            collective_id=0, has_side_effects=True, vmem_limit_bytes=48 << 20
        ),
    )(tokens, w_up, w_down, grad_out)


def solution(mesh):
    spec = P(("depth", "row"), "col")
    return jax.shard_map(
        local, mesh=mesh, in_specs=(spec,) * 4, out_specs=(spec,) * 4, check_vma=False
    )
```

time: 868 us -> 83.6 us (0.10)
  blocking collectives: 691 us -> 0 us
  waiting for transfers between devices: 141 us -> 0 us
  Pallas kernels: 0 us -> 75.5 us
  between operations: 14.8 us -> 0.65 us
  matrix products: 9.34 us -> 0 us
    unnamed x1 -> x0, blocking collectives: 446 us -> none
    all_gather x2 -> x0, blocking collectives: 244 us -> none  [the longest x1 130 us: local(): lax.all_gather(grad_out, ('depth', 'row'), axis=0, tiled=True)]
    psum x1 -> x0, waiting for transfers between devices: 141 us -> none  [local(): lax.psum(along_rows(tok_all, w_up).astype(jnp.bfloat16), 'col')]
    pallas_call x0 -> x1, Pallas kernels: none -> 75.5 us  [local(): pl.pallas_call(functools.partial(kernel, scale), name='ffn', out_shape=(s...]
    dot_general x6 -> x0, matrix products: 9.34 us -> none  [the longest x2 3.49 us: spread_sum(): jnp.dot(hidden_rows, weight, preferred_element_type=jnp.float32)]
  transfers between devices with their start and end apart: 1 -> 0, of which waited for: 1 -> 0; matrix products, arithmetic and copies ran while one was open for 0% -> 0% of each run, Pallas kernels for 0% -> 0%
where the time goes in v1:
time: 83.6 us; the launch traced here: 83.3 us
  Pallas kernels  75.5 us (90%)
  local copies, waits for them, and re-layouts  7.17 us (9%)
    pallas_call x1, Pallas kernels, local(): pl.pallas_call(functools.partial(kernel, scale), name='ffn', out_shape=(s...  75.5 us
    unnamed x12, local copies, waits for them, and re-layouts  7.17 us

profile of v1, /device:TPU:1, one launch (start us, length us, event | category | flops | bytes accessed | tf_op | source)
XLA Modules:
  0.0 83.3 jit_solution(6632799158508098120)
XLA Ops:
  0.6 0.0 copy-start
  0.6 1.3 %copy-done = bf16[384,1536]{1,0:T(8,128)(2,1)S(1)} copy-done((bf16[384,1536]{1,0:T(8,128)(2,1)S(1)}, bf16[384,1536]{1,0:T(8,128)(2,1)}, u32[]{:S(2)}) %copy-start) | copy-done | bytes 1179672
  1.9 0.0 copy-start.1
  1.9 1.3 %copy-done.1 = bf16[384,1536]{1,0:T(8,128)(2,1)S(1)} copy-done((bf16[384,1536]{1,0:T(8,128)(2,1)S(1)}, bf16[384,1536]{1,0:T(8,128)(2,1)}, u32[]{:S(2)}) %copy-start.1) | copy-done | bytes 1179672
  3.2 0.0 copy-start.2
  3.2 0.7 copy-done.2
  3.9 0.0 copy-start.3
  3.9 0.7 copy-done.3
  4.6 75.5 %ffn.1 = (bf16[4,1536]{1,0:T(4,128)(2,1)S(1)}, bf16[4,1536]{1,0:T(4,128)(2,1)S(1)}, bf16[384,1536]{1,0:T(8,128)(2,1)S(1)}, bf16[384,1536]{1,0:T(8,128)(2,1)S(1)}) custom-call(bf16[4,1536]{1,0:T(4,128)(2,1)S(1)} %copy-done.2, bf16[384,1536]{1,0:T(8,128)(2,1)S(1)} %copy-done, bf16[384,1536]{1,0:T(8,128)(2,1)S(1)} %copy-done.1, bf16[4,1536]{1,0:T(4,128)(2,1)S(1)} %copy-done.3), custom_call_target="tpu_custom_call" | custom-call | tf_op jit(solution)/shard_map/ffn/pallas_call | solution.py:212
  80.1 0.6 copy.12
  80.7 0.6 copy.13
  81.3 1.0 %copy.14 = bf16[384,1536]{1,0:T(8,128)(2,1)} copy(bf16[384,1536]{1,0:T(8,128)(2,1)S(1)} %get-tuple-element.10) | data formatting | bytes 2359296
  82.3 1.0 %copy.15 = bf16[384,1536]{1,0:T(8,128)(2,1)} copy(bf16[384,1536]{1,0:T(8,128)(2,1)S(1)} %get-tuple-element.11) | data formatting | bytes 2359296
Async XLA Ops:
  0.6 1.3 %copy-start = (bf16[384,1536]{1,0:T(8,128)(2,1)S(1)}, bf16[384,1536]{1,0:T(8,128)(2,1)}, u32[]{:S(2)}) copy-start(bf16[384,1536]{1,0:T(8,128)(2,1)} %w_up_ref.1) | copy-start | bytes 3538948
  1.9 1.3 %copy-start.1 = (bf16[384,1536]{1,0:T(8,128)(2,1)S(1)}, bf16[384,1536]{1,0:T(8,128)(2,1)}, u32[]{:S(2)}) copy-start(bf16[384,1536]{1,0:T(8,128)(2,1)} %w_down_ref.1) | copy-start | bytes 3538948
  3.2 0.7 copy-start.2
  3.9 0.7 copy-start.3

commit v2 on v1

v2 whole, which is shorter than its diff:
```python
import functools
import math

import jax
import jax.numpy as jnp
from jax import lax
from jax.experimental import pallas as pl
from jax.experimental.pallas import tpu as pltpu
from jax.sharding import PartitionSpec as P

MESH = pl.DeviceIdType.MESH
NX, NY, NZ = 4, 4, 8
F32, BF16 = jnp.float32, jnp.bfloat16
coeff = 0.7978845608028654


def gelu_value(value):
    inner = jnp.tanh(coeff * (value + 0.044715 * value * value * value))
    return 0.5 * value * (1.0 + inner)


def gelu_slope(value):
    inner = jnp.tanh(coeff * (value + 0.044715 * value * value * value))
    return 0.5 * (1.0 + inner) + 0.5 * value * (1.0 - inner * inner) * coeff * (
        1.0 + 3.0 * 0.044715 * value * value
    )


def along_rows(left, right):
    return lax.dot_general(left, right, (((1,), (1,)), ((), ())), preferred_element_type=F32)


def over_tokens(left, right):
    return lax.dot_general(left, right, (((0,), (0,)), ((), ())), preferred_element_type=F32)


def kernel(
    scale,
    tok_ref, w_up_ref, w_down_ref, grad_ref,
    out_ref, gin_ref, gwu_ref, gwd_ref,
    rows_in, weights, pieces, full, part, xin, far_out, far_in, hidden,
    core_out, core_in, y_out, y_in, z_out, z_in, last_out, last_in,
    r_sem, w_sem, az, ay, ac, xr, fz, xa, rc, ry, rz, rl,
):
    depth, row, col = lax.axis_index("depth"), lax.axis_index("row"), lax.axis_index("col")
    z, y, core, x = depth, row // 2, row % 2, col % NX

    def at(z=depth, y=y, core=core, col=col):
        return {"depth": z, "row": y * 2 + core, "col": col}

    half = z // 4
    near_z = [4 * half + (z + k) % 4 for k in (2, 1, 3)]
    far_z = [4 * (1 - half) + (z + k) % 4 for k in range(4)]
    z_peers = [*far_z, *near_z]
    y_peers = [(y + k) % NY for k in (2, 1, 3)]
    x_peers = [(x + k) % NX for k in (2, 1, 3)]
    y_order = (y_peers[1], y_peers[2], y_peers[0])
    x_order = (x_peers[1], x_peers[2], x_peers[0])
    along_z = [at(z=p) for p in z_peers]
    along_y = [at(y=p) for p in y_peers]
    along_x = [at(col=col - x + p) for p in x_peers]
    other = at(core=1 - core)
    far = at(col=(col + NX) % (2 * NX))

    barrier = pltpu.get_barrier_semaphore()
    everyone = [far, *along_z, *along_y, *along_x, other]
    for d in everyone:
        pl.semaphore_signal(barrier, inc=1, device_id=d, device_id_type=MESH)
    row_loads = [pltpu.make_async_copy(ref, rows_in.at[i], r_sem.at[i]) for i, ref in enumerate((tok_ref, grad_ref))]
    loads = [pltpu.make_async_copy(ref, weights.at[i], w_sem.at[i]) for i, ref in enumerate((w_up_ref, w_down_ref))]
    for c in (*row_loads, *loads):
        c.start()

    def copy(src, dst, sems, send_at, recv_at, to):
        return pltpu.make_async_remote_copy(
            src_ref=src, dst_ref=dst, send_sem=sems.at[(0, *send_at)], recv_sem=sems.at[(1, *recv_at)],
            device_id=to, device_id_type=MESH,
        )

    started = []

    def send(*args):
        c = copy(*args)
        c.start()
        started.append(c)

    def arrive(dst, sems, recv_at):
        copy(dst, dst, sems, recv_at, recv_at, other).wait_recv()

    for s in range(2):
        row_loads[s].wait()
        v = rows_in[s].astype(F32)
        folded = jnp.concatenate([v[:, 384 * c : 384 * (c + 1)] for c in range(4)], axis=0)
        pieces[s, y, core, z] = folded.astype(BF16)
    pl.semaphore_wait(barrier, len(everyone))

    for s in range(2):
        mine = pieces.at[s, y, core, z]
        for p, d in zip(z_peers, along_z, strict=True):
            send(mine, mine, az, (s, p), (s, z), d)

    def part_of(s, q, k, h):
        return pieces.at[s, q, k, pl.ds(4 * (half if h == 0 else 1 - half), 4)]

    def over_y(s, h):
        for p in near_z if h == 0 else reversed(far_z):
            arrive(pieces.at[s, y, core, p], az, (s, p))
        mine = part_of(s, y, core, h)
        for p, d in zip(y_peers, along_y, strict=True):
            send(mine, mine, ay, (s, h, p), (s, h, y), d)
        send(mine, mine, ac, (s, h, y), (s, h, y), other)

    def pass_on(s, h):
        for p in y_order:
            block = part_of(s, p, core, h)
            arrive(block, ay, (s, h, p))
            send(block, block, ac, (s, h, p), (s, h, p), other)

    top = lax.broadcasted_iota(jnp.int32, (NZ, 8, 384), 1) < 4

    def block_of(s, q):
        for h in range(2):
            arrive(part_of(s, q, 1 - core, h), ac, (s, h, q))
        halves = [pieces[s, q, k].astype(F32).reshape(NZ, 2, 8, 384) for k in range(2)]
        rows = pl.ds(pl.multiple_of(64 * q, 64), 64)
        for c in range(4):
            first, second = halves[0][:, c // 2], halves[1][:, c // 2]
            if c % 2 == 0:
                block = jnp.where(top, first, pltpu.roll(second, 4, 1))
            else:
                block = jnp.where(top, pltpu.roll(first, 4, 1), second)
            full[s, rows, 384 * c : 384 * (c + 1)] = block.reshape(64, 384).astype(BF16)
        part[s, q] = along_rows(full[s, rows, :], weights[s]).astype(BF16)

        @pl.when(q != x)
        def _():
            copy(part.at[s, q], xin.at[s, x], xr, (s, q), (s, x), at(col=col - x + q)).start()

    over_y(0, 0)
    over_y(0, 1)
    over_y(1, 0)
    pass_on(0, 0)
    over_y(1, 1)
    loads[0].wait()
    block_of(0, y)
    pass_on(0, 1)
    for p in y_order:
        block_of(0, p)
    pass_on(1, 0)
    loads[1].wait()
    block_of(1, y)
    pass_on(1, 1)
    for p in y_order:
        block_of(1, p)

    for s in range(2):
        total = part[s, x].astype(F32)
        for p in x_order:
            arrive(xin.at[s, p], xr, (s, p))
            total += xin[s, p].astype(F32)
        far_out[s] = total.astype(BF16)
        send(far_out.at[s], far_in.at[s], fz, (s,), (s,), far)

    own = pl.multiple_of(core * 768, 128)
    not_own = pl.multiple_of((1 - core) * 768, 128)

    def summed(s):
        arrive(far_in.at[s], fz, (s,))
        return far_out[s].astype(F32) + far_in[s].astype(F32)

    def over_x(s, value):
        hidden[s, x] = value.astype(BF16)
        mine = hidden.at[s, x]
        for p, d in zip(x_peers, along_x, strict=True):
            send(mine, mine, xa, (s, p), (s, x), d)

    def to_core(s):
        for p in x_order:
            arrive(hidden.at[s, p], xa, (s, p))
        h = hidden[s].reshape(256, 384)
        core_out[s] = jnp.dot(h, weights[1 - s, :, pl.ds(not_own, 768)], preferred_element_type=F32).astype(BF16)
        send(core_out.at[s], core_in.at[s], rc, (s,), (s,), other)

    def to_y(s):
        h = hidden[s].reshape(256, 384)
        part_out = jnp.dot(h, weights[1 - s, :, pl.ds(own, 768)], preferred_element_type=F32)
        arrive(core_in.at[s], rc, (s,))
        y_out[s] = (part_out + core_in[s].astype(F32)).astype(BF16).reshape(NY, 64, 768)
        for p, d in zip(y_peers, along_y, strict=True):
            send(y_out.at[s, p], y_in.at[s, y], ry, (s, p), (s, y), d)

    def weight_grad(s, ref):
        h = hidden[1 - s].reshape(256, 384)
        for c in range(4):
            cols = slice(384 * c, 384 * (c + 1))
            ref[:, cols] = (over_tokens(h, full[s, :, cols]) * scale).astype(BF16)

    def to_z(s):
        total = y_out[s, y].astype(F32)
        for p in y_order:
            arrive(y_in.at[s, p], ry, (s, p))
            total += y_in[s, p].astype(F32)
        rows = total.reshape(NZ, 8, 768)
        z_out[s] = jnp.concatenate([rows[:, :, :384], rows[:, :, 384:]], axis=1).astype(BF16)
        for p, d in zip(z_peers, along_z, strict=True):
            send(z_out.at[s, p], z_in.at[s, z], rz, (s, p), (s, z), d)

    def to_last(s):
        total = z_out[s, z].astype(F32)
        for p in (*near_z, *far_z):
            arrive(z_in.at[s, p], rz, (s, p))
            total += z_in[s, p].astype(F32)
        last_out[s] = total.astype(BF16)
        send(last_out.at[s], last_in.at[s], rl, (s,), (s,), other)

    def finish(s, ref):
        arrive(last_in.at[s], rl, (s,))
        mine, theirs = last_out[s].astype(F32), last_in[s].astype(F32)
        left = jnp.where(core == 0, mine, theirs)
        right = jnp.where(core == 0, theirs, mine)
        rows = jnp.concatenate([left[:8], left[8:], right[:8], right[8:]], axis=1)
        ref[...] = jnp.where(core == 0, rows[:4], rows[4:]).astype(BF16)

    pre = summed(0)
    over_x(0, gelu_value(pre))
    slope = gelu_slope(pre)
    to_core(0)
    over_x(1, summed(1) * slope)
    to_y(0)
    to_core(1)
    to_y(1)
    weight_grad(1, gwd_ref)
    to_z(0)
    weight_grad(0, gwu_ref)
    to_z(1)
    to_last(0)
    finish(0, out_ref)
    to_last(1)
    finish(1, gin_ref)
    for c in started:
        c.wait_send()
    for s in range(2):
        for p in x_peers:
            copy(part.at[s, p], xin.at[s, x], xr, (s, p), (s, x), other).wait_send()


def write_out(*refs):
    sources, targets, sem = refs[:4], refs[4:8], refs[8]
    copies = [pltpu.make_async_copy(a, b, sem.at[i]) for i, (a, b) in enumerate(zip(sources, targets, strict=True))]
    for c in copies:
        c.start()
    for c in copies:
        c.wait()


def local(tokens, w_up, w_down, grad_out):
    n_tokens = tokens.shape[0] * lax.axis_size("depth") * lax.axis_size("row")
    scale = 1.0 / math.sqrt(n_tokens)
    vmem, hbm = pl.BlockSpec(memory_space=pltpu.VMEM), pl.BlockSpec(memory_space=pltpu.HBM)
    dma = pltpu.SemaphoreType.DMA
    shape = jax.ShapeDtypeStruct
    shapes = (
        shape((4, 1536), BF16), shape((4, 1536), BF16), shape((384, 1536), BF16), shape((384, 1536), BF16),
    )
    held = pltpu.with_memory_space_constraint
    results = pl.pallas_call(
        functools.partial(kernel, scale),
        name="ffn",
        out_shape=tuple(pltpu.VMEM(a.shape, a.dtype) for a in shapes),
        in_specs=[hbm] * 4,
        out_specs=(vmem,) * 4,
        scratch_shapes=[
            pltpu.VMEM((2, 4, 1536), BF16),
            pltpu.VMEM((2, 384, 1536), BF16),
            pltpu.VMEM((2, NY, 2, NZ, 16, 384), BF16),
            pltpu.VMEM((2, 256, 1536), BF16),
            pltpu.VMEM((2, NX, 64, 384), BF16),
            pltpu.VMEM((2, NX, 64, 384), BF16),
            pltpu.VMEM((2, 64, 384), BF16),
            pltpu.VMEM((2, 64, 384), BF16),
            pltpu.VMEM((2, NX, 64, 384), BF16),
            pltpu.VMEM((2, 256, 768), BF16),
            pltpu.VMEM((2, 256, 768), BF16),
            pltpu.VMEM((2, NY, 64, 768), BF16),
            pltpu.VMEM((2, NY, 64, 768), BF16),
            pltpu.VMEM((2, NZ, 16, 384), BF16),
            pltpu.VMEM((2, NZ, 16, 384), BF16),
            pltpu.VMEM((2, 16, 384), BF16),
            pltpu.VMEM((2, 16, 384), BF16),
            dma((2,)), dma((2,)),
            dma((2, 2, NZ)), dma((2, 2, 2, NY)), dma((2, 2, 2, NY)), dma((2, 2, NX)), dma((2, 2)), dma((2, 2, NX)),
            dma((2, 2)), dma((2, 2, NY)), dma((2, 2, NZ)), dma((2, 2)),
        ],
        compiler_params=pltpu.CompilerParams(
            collective_id=0, has_side_effects=True, vmem_limit_bytes=48 << 20
        ),
    )(*(held(a, pltpu.HBM) for a in (tokens, w_up, w_down, grad_out)))
    return pl.pallas_call(
        write_out,
        name="write_out",
        out_shape=tuple(pltpu.HBM(a.shape, a.dtype) for a in shapes),
        in_specs=[vmem] * 4,
        out_specs=(hbm,) * 4,
        scratch_shapes=[dma((4,))],
    )(*(held(a, pltpu.VMEM) for a in results))


def solution(mesh):
    spec = P(("depth", "row"), "col")
    return jax.shard_map(
        local, mesh=mesh, in_specs=(spec,) * 4, out_specs=(spec,) * 4, check_vma=False
    )
```

time: 83.6 us -> 76 us (0.909)
  local copies, waits for them, and re-layouts: 7.17 us -> 0 us
    unnamed x12 -> x0, local copies, waits for them, and re-layouts: 7.17 us -> none
    pallas_call x1 -> x2, Pallas kernels: 75.5 us -> 75.2 us  [the longest x1 73.8 us: local(): pl.pallas_call(functools.partial(kernel, scale), name='ffn', out_shape=tu...]
where the time goes in v2:
time: 76 us; the launch traced here: 75.9 us
  Pallas kernels  75.2 us (99%)
    pallas_call x1, Pallas kernels, local(): pl.pallas_call(functools.partial(kernel, scale), name='ffn', out_shape=tu...  73.8 us

profile of v2, /device:TPU:1, one launch (start us, length us, event | category | flops | bytes accessed | tf_op | source)
XLA Modules:
  0.0 75.9 jit_solution(4462746412592875063)
XLA Ops:
  0.6 73.8 %ffn.1 = (bf16[4,1536]{1,0:T(4,128)(2,1)S(1)}, bf16[4,1536]{1,0:T(4,128)(2,1)S(1)}, bf16[384,1536]{1,0:T(8,128)(2,1)S(1)}, bf16[384,1536]{1,0:T(8,128)(2,1)S(1)}) custom-call(bf16[4,1536]{1,0:T(4,128)(2,1)} %tok_ref.1, bf16[384,1536]{1,0:T(8,128)(2,1)} %w_up_ref.1, bf16[384,1536]{1,0:T(8,128)(2,1)} %w_down_ref.1, bf16[4,1536]{1,0:T(4,128)(2,1)} %grad_ref.1), custom_call_target="tpu_custom_call" | custom-call | tf_op jit(solution)/shard_map/ffn/pallas_call | solution.py:266
  74.4 1.4 %write_out.1 = (bf16[4,1536]{1,0:T(4,128)(2,1)}, bf16[4,1536]{1,0:T(4,128)(2,1)}, bf16[384,1536]{1,0:T(8,128)(2,1)}, bf16[384,1536]{1,0:T(8,128)(2,1)}) custom-call(bf16[4,1536]{1,0:T(4,128)(2,1)S(1)} %get-tuple-element.8.refs_0_, bf16[4,1536]{1,0:T(4,128)(2,1)S(1)} %get-tuple-element.9.refs_1_, bf16[384,1536]{1,0:T(8,128)(2,1)S(1)} %get-tuple-element.10.refs_2_, ...), custom_call_target="tpu_custom_call" | custom-call | tf_op jit(solution)/shard_map/write_out/pallas_call | solution.py:298

commit v3 on v2

v3 whole, which is shorter than its diff:
```python
import functools
import math

import jax
import jax.numpy as jnp
from jax import lax
from jax.experimental import pallas as pl
from jax.experimental.pallas import tpu as pltpu
from jax.sharding import PartitionSpec as P

MESH = pl.DeviceIdType.MESH
NX, NY, NZ = 4, 4, 8
F32, BF16 = jnp.float32, jnp.bfloat16
coeff = 0.7978845608028654


def gelu_value(value):
    inner = jnp.tanh(coeff * (value + 0.044715 * value * value * value))
    return 0.5 * value * (1.0 + inner)


def gelu_slope(value):
    inner = jnp.tanh(coeff * (value + 0.044715 * value * value * value))
    return 0.5 * (1.0 + inner) + 0.5 * value * (1.0 - inner * inner) * coeff * (
        1.0 + 3.0 * 0.044715 * value * value
    )


def along_rows(left, right):
    return lax.dot_general(left, right, (((1,), (1,)), ((), ())), preferred_element_type=F32)


def over_tokens(left, right):
    return lax.dot_general(left, right, (((0,), (0,)), ((), ())), preferred_element_type=F32)


def kernel(
    scale,
    tok_ref, w_up_ref, w_down_ref, grad_ref,
    out_ref, gin_ref, gwu_ref, gwd_ref,
    rows_in, weights, lent, pieces, full, part, xin, far_out, far_in, slopes_out, slopes, hidden,
    y_out, y_in, z_out, z_in, last_out, last_in,
    r_sem, w_sem, wx, cx, az, ay, fx, xr, fz, sx, xa, hx, ry, rz, lx,
):
    depth, row, col = lax.axis_index("depth"), lax.axis_index("row"), lax.axis_index("col")
    z, y, core, x = depth, row // 2, row % 2, col % NX

    def at(z=depth, y=y, core=core, col=col):
        return {"depth": z, "row": y * 2 + core, "col": col}

    half = z // 4
    near_z = [4 * half + (z + k) % 4 for k in (2, 1, 3)]
    far_z = [4 * (1 - half) + (z + k) % 4 for k in range(4)]
    z_peers = [*far_z, *near_z]
    y_peers = [(y + k) % NY for k in (2, 1, 3)]
    x_peers = [(x + k) % NX for k in (2, 1, 3)]
    y_order = (y_peers[1], y_peers[2], y_peers[0])
    x_order = (x_peers[1], x_peers[2], x_peers[0])
    along_z = [at(z=p) for p in z_peers]
    along_y = [at(y=p) for p in y_peers]
    along_x = [at(col=col - x + p) for p in x_peers]
    other = at(core=1 - core)
    far = at(col=(col + NX) % (2 * NX))

    barrier = pltpu.get_barrier_semaphore()
    everyone = [far, *along_z, *along_y, *along_x, other]
    for d in everyone:
        pl.semaphore_signal(barrier, inc=1, device_id=d, device_id_type=MESH)
    row_loads = [pltpu.make_async_copy(ref, rows_in.at[i], r_sem.at[i]) for i, ref in enumerate((tok_ref, grad_ref))]
    loads = [pltpu.make_async_copy(ref, weights.at[i, core], w_sem.at[i]) for i, ref in enumerate((w_up_ref, w_down_ref))]
    for c in (*row_loads, *loads):
        c.start()

    def copy(src, dst, sems, send_at, recv_at, to):
        return pltpu.make_async_remote_copy(
            src_ref=src, dst_ref=dst, send_sem=sems.at[(0, *send_at)], recv_sem=sems.at[(1, *recv_at)],
            device_id=to, device_id_type=MESH,
        )

    started = []

    def send(*args):
        c = copy(*args)
        c.start()
        started.append(c)

    def arrive(dst, sems, recv_at):
        copy(dst, dst, sems, recv_at, recv_at, other).wait_recv()

    for c in row_loads:
        c.wait()

    def folded(s):
        v = rows_in[s].astype(F32)
        return jnp.concatenate([v[:, 384 * c : 384 * (c + 1)] for c in range(4)], axis=0).astype(BF16)

    pieces[core, y, z] = folded(core)
    lent[...] = folded(1 - core)
    pl.semaphore_wait(barrier, len(everyone))

    send(lent, pieces.at[core, y, z], cx, (), (), other)
    for a in range(2):
        mine = pieces.at[a, y, z]

        @pl.when(core != a)
        def _():
            arrive(mine, cx, ())

        for p, d in zip(z_peers, along_z, strict=True):
            send(mine, mine, az, (a, p), (a, z), d)
    for i, ref in enumerate((w_up_ref, w_down_ref)):
        send(ref, weights.at[i, core], wx, (i,), (i,), other)

    def part_of(k, q):
        return pieces.at[k // 2, q, pl.ds(4 * (half if k % 2 == 0 else 1 - half), 4)]

    def over_y(k):
        a = k // 2
        for p in near_z if k % 2 == 0 else reversed(far_z):
            arrive(pieces.at[a, y, p], az, (a, p))
        block = part_of(k, y)
        for p, d in zip(y_peers, along_y, strict=True):
            send(block, block, ay, (k, p), (k, y), d)

    top = lax.broadcasted_iota(jnp.int32, (2, 8, 384), 1) < 4

    def order(k, q):
        v = part_of(k, q)[...].astype(F32).reshape(2, 2, 2, 8, 384)
        rows = pl.ds(pl.multiple_of(16 * q, 16), 16)
        for c in range(4):
            first, second = v[:, 0, c // 2], v[:, 1, c // 2]
            if c % 2 == 0:
                block = jnp.where(top, first, pltpu.roll(second, 4, 1))
            else:
                block = jnp.where(top, pltpu.roll(first, 4, 1), second)
            full[core, k, rows, 384 * c : 384 * (c + 1)] = block.reshape(16, 384).astype(BF16)

    def project(k):
        order(k, y)
        for p in y_order:
            arrive(part_of(k, p), ay, (k, p))
            order(k, p)
        if k == 0:
            for i in range(2):
                loads[i].wait()
                arrive(weights.at[i, 1 - core], wx, (i,))
        for f in range(2):
            part[k, :, f] = along_rows(full[core, k], weights[core, f]).astype(BF16).reshape(NX, 16, 384)
        for p, d in zip(x_peers, along_x, strict=True):
            send(part.at[k, p], xin.at[k, x], xr, (k, p), (k, x), d)
        send(full.at[core, k], full.at[core, k], fx, (k,), (k,), other)

    def to_far(a):
        total = part[a, x].astype(F32)
        for p in x_order:
            arrive(xin.at[a, p], xr, (a, p))
            total += xin[a, p].astype(F32)
        far_out[a] = total.astype(BF16)
        send(far_out.at[a], far_in.at[a], fz, (a,), (a,), far)

    def slope_copy(a):
        return copy(slopes_out.at[a], slopes.at[a], sx, (a,), (a,), other)

    def activate(a):
        arrive(far_in.at[a], fz, (a,))

        @pl.when(core == 0)
        def _():
            pre = far_out[a].astype(F32) + far_in[a].astype(F32)
            slopes_out[a] = gelu_slope(pre)
            slope_copy(a).start()
            hidden[core, a, x] = gelu_value(pre).astype(BF16)

        @pl.when(core == 1)
        def _():
            slope_copy(a).wait_recv()
            grad_act = far_out[a].astype(F32) + far_in[a].astype(F32)
            hidden[core, a, x] = (grad_act * slopes[a]).astype(BF16)

        block = hidden.at[core, a, x]
        for p, d in zip(x_peers, along_x, strict=True):
            send(block, block, xa, (a, p), (a, x), d)

    def back(a):
        for p in x_order:
            arrive(hidden.at[core, a, p], xa, (a, p))
        for n in range(2):
            cols = slice(768 * n, 768 * (n + 1))
            total = sum(
                jnp.dot(
                    hidden[core, a, :, f].reshape(64, 384), weights[1 - core, f, :, cols], preferred_element_type=F32
                )
                for f in range(2)
            )
            y_out[a, :, :, cols] = total.astype(BF16).reshape(NY, 16, 768)
        for p, d in zip(y_peers, along_y, strict=True):
            send(y_out.at[a, p], y_in.at[a, y], ry, (a, p), (a, y), d)
        lend = hidden.at[core, a, :, 1 - core]
        send(lend, lend, hx, (a,), (a,), other)

    def to_z(k):
        total = y_out[k, y].astype(F32)
        for p in y_order:
            arrive(y_in.at[k, p], ry, (k, p))
            total += y_in[k, p].astype(F32)
        rows = total.reshape(2, 8, 1536)
        c = [rows[:, :, 384 * i : 384 * (i + 1)] for i in range(4)]
        for parity in range(2):
            tiles = [
                jnp.where(top, c[2 * r], pltpu.roll(c[2 * r + 1], 4, 1))
                if parity == 0
                else jnp.where(top, pltpu.roll(c[2 * r], 4, 1), c[2 * r + 1])
                for r in range(2)
            ]
            z_out[k, :, parity] = jnp.concatenate(tiles, axis=1).astype(BF16)
        a = k // 2
        for p in near_z if k % 2 == 0 else far_z:
            send(z_out.at[k, p % 4 // 2, p % 2], z_in.at[a, z], rz, (a, p), (a, z), at(z=p))
        if k % 2 == 0:
            z_in[a, z] = z_out[k, z % 4 // 2, z % 2]

    def unfolded(v):
        low, high = v[:8], v[8:]
        return jnp.concatenate([low, pltpu.roll(low, 4, 0), high, pltpu.roll(high, 4, 0)], axis=1)[:4]

    last_copy = copy(last_out, last_in, lx, (), (), other)

    def finish(a, own_ref):
        for p in (*near_z, *far_z):
            arrive(z_in.at[a, p], rz, (a, p))
        total = sum(z_in[a, i].astype(F32) for i in range(NZ))

        @pl.when(core == a)
        def _():
            own_ref[...] = unfolded(total).astype(BF16)

        @pl.when(core != a)
        def _():
            last_out[...] = total.astype(BF16)
            last_copy.start()

    def weight_grad(s, ref):
        h = hidden[1 - s, :, :, core].reshape(256, 384)
        for c in range(4):
            cols = slice(384 * c, 384 * (c + 1))
            ref[:, cols] = (over_tokens(h, full[s, :, :, cols].reshape(256, 384)) * scale).astype(BF16)

    for k in range(4):
        over_y(k)
    project(0)
    project(1)
    to_far(0)
    project(2)
    to_far(1)
    project(3)
    to_far(2)
    to_far(3)
    activate(0)
    activate(1)
    activate(2)
    back(0)
    activate(3)
    back(1)
    back(2)
    to_z(0)
    back(3)
    to_z(1)
    to_z(2)
    to_z(3)
    for k in range(4):
        arrive(full.at[1 - core, k], fx, (k,))
        arrive(hidden.at[1 - core, k, :, core], hx, (k,))
    weight_grad(0, gwu_ref)
    weight_grad(1, gwd_ref)
    finish(0, out_ref)
    finish(1, gin_ref)
    last_copy.wait()
    theirs = unfolded(last_in[...].astype(F32)).astype(BF16)

    @pl.when(core == 0)
    def _():
        gin_ref[...] = theirs
        for k in range(4):
            slope_copy(k).wait_send()

    @pl.when(core == 1)
    def _():
        out_ref[...] = theirs

    for c in started:
        c.wait_send()


def write_out(*refs):
    sources, targets, sem = refs[:4], refs[4:8], refs[8]
    copies = [pltpu.make_async_copy(a, b, sem.at[i]) for i, (a, b) in enumerate(zip(sources, targets, strict=True))]
    for c in copies:
        c.start()
    for c in copies:
        c.wait()


def local(tokens, w_up, w_down, grad_out):
    n_tokens = tokens.shape[0] * lax.axis_size("depth") * lax.axis_size("row")
    scale = 1.0 / math.sqrt(n_tokens)
    vmem, hbm = pl.BlockSpec(memory_space=pltpu.VMEM), pl.BlockSpec(memory_space=pltpu.HBM)
    dma = pltpu.SemaphoreType.DMA
    shape = jax.ShapeDtypeStruct
    shapes = (
        shape((4, 1536), BF16), shape((4, 1536), BF16), shape((384, 1536), BF16), shape((384, 1536), BF16),
    )
    held = pltpu.with_memory_space_constraint
    results = pl.pallas_call(
        functools.partial(kernel, scale),
        name="ffn",
        out_shape=tuple(pltpu.VMEM(a.shape, a.dtype) for a in shapes),
        in_specs=[hbm] * 4,
        out_specs=(vmem,) * 4,
        scratch_shapes=[
            pltpu.VMEM((2, 4, 1536), BF16),
            pltpu.VMEM((2, 2, 384, 1536), BF16),
            pltpu.VMEM((16, 384), BF16),
            pltpu.VMEM((2, NY, NZ, 16, 384), BF16),
            pltpu.VMEM((2, 4, 64, 1536), BF16),
            pltpu.VMEM((4, NX, 2, 16, 384), BF16),
            pltpu.VMEM((4, NX, 2, 16, 384), BF16),
            pltpu.VMEM((4, 2, 16, 384), BF16),
            pltpu.VMEM((4, 2, 16, 384), BF16),
            pltpu.VMEM((4, 2, 16, 384), F32),
            pltpu.VMEM((4, 2, 16, 384), F32),
            pltpu.VMEM((2, 4, NX, 2, 16, 384), BF16),
            pltpu.VMEM((4, NY, 16, 1536), BF16),
            pltpu.VMEM((4, NY, 16, 1536), BF16),
            pltpu.VMEM((4, 2, 2, 16, 384), BF16),
            pltpu.VMEM((2, NZ, 16, 384), BF16),
            pltpu.VMEM((16, 384), BF16),
            pltpu.VMEM((16, 384), BF16),
            dma((2,)), dma((2,)), dma((2, 2)), dma((2,)),
            dma((2, 2, NZ)), dma((2, 4, NY)), dma((2, 4)), dma((2, 4, NX)), dma((2, 4)), dma((2, 4)), dma((2, 4, NX)),
            dma((2, 4)), dma((2, 4, NY)), dma((2, 2, NZ)), dma((2,)),
        ],
        compiler_params=pltpu.CompilerParams(
            collective_id=0, has_side_effects=True, vmem_limit_bytes=48 << 20
        ),
    )(*(held(a, pltpu.HBM) for a in (tokens, w_up, w_down, grad_out)))
    return pl.pallas_call(
        write_out,
        name="write_out",
        out_shape=tuple(pltpu.HBM(a.shape, a.dtype) for a in shapes),
        in_specs=[vmem] * 4,
        out_specs=(hbm,) * 4,
        scratch_shapes=[dma((4,))],
    )(*(held(a, pltpu.VMEM) for a in results))


def solution(mesh):
    spec = P(("depth", "row"), "col")
    return jax.shard_map(
        local, mesh=mesh, in_specs=(spec,) * 4, out_specs=(spec,) * 4, check_vma=False
    )
```

time: 76 us -> 70.4 us (0.926)
  Pallas kernels: 75.2 us -> 69.6 us
    pallas_call x1, Pallas kernels: 73.8 us -> 68.1 us  [local(): pl.pallas_call(functools.partial(kernel, scale), name='ffn', out_shape=tu...]
where the time goes in v3:
time: 70.4 us; the launch traced here: 70.2 us
  Pallas kernels  69.6 us (99%)
    pallas_call x1, Pallas kernels, local(): pl.pallas_call(functools.partial(kernel, scale), name='ffn', out_shape=tu...  68.1 us
    pallas_call x1, Pallas kernels, local(): pl.pallas_call(write_out, name='write_out', out_shape=tuple((pltpu.HBM(a....  1.45 us

profile of v3, /device:TPU:1, one launch (start us, length us, event | category | flops | bytes accessed | tf_op | source)
XLA Modules:
  0.0 70.2 jit_solution(3936605925430882912)
XLA Ops:
  0.6 68.1 %ffn.1 = (bf16[4,1536]{1,0:T(4,128)(2,1)S(1)}, bf16[4,1536]{1,0:T(4,128)(2,1)S(1)}, bf16[384,1536]{1,0:T(8,128)(2,1)S(1)}, bf16[384,1536]{1,0:T(8,128)(2,1)S(1)}) custom-call(bf16[4,1536]{1,0:T(4,128)(2,1)} %tok_ref.1, bf16[384,1536]{1,0:T(8,128)(2,1)} %w_up_ref.1, bf16[384,1536]{1,0:T(8,128)(2,1)} %w_down_ref.1, bf16[4,1536]{1,0:T(4,128)(2,1)} %grad_ref.1), custom_call_target="tpu_custom_call" | custom-call | tf_op jit(solution)/shard_map/ffn/pallas_call | solution.py:313
  68.8 1.4 %write_out.1 = (bf16[4,1536]{1,0:T(4,128)(2,1)}, bf16[4,1536]{1,0:T(4,128)(2,1)}, bf16[384,1536]{1,0:T(8,128)(2,1)}, bf16[384,1536]{1,0:T(8,128)(2,1)}) custom-call(bf16[4,1536]{1,0:T(4,128)(2,1)S(1)} %get-tuple-element.8.refs_0_, bf16[4,1536]{1,0:T(4,128)(2,1)S(1)} %get-tuple-element.9.refs_1_, bf16[384,1536]{1,0:T(8,128)(2,1)S(1)} %get-tuple-element.10.refs_2_, ...), custom_call_target="tpu_custom_call" | custom-call | tf_op jit(solution)/shard_map/write_out/pallas_call | solution.py:346

commit v4 on v3

--- a/solution.py
+++ b/solution.py
@@ -39,8 +39,8 @@
     tok_ref, w_up_ref, w_down_ref, grad_ref,
     out_ref, gin_ref, gwu_ref, gwd_ref,
     rows_in, weights, lent, pieces, full, part, xin, far_out, far_in, slopes_out, slopes, hidden,
-    y_out, y_in, z_out, z_in, last_out, last_in,
-    r_sem, w_sem, wx, cx, az, ay, fx, xr, fz, sx, xa, hx, ry, rz, lx,
+    y_out, y_in, z_out, z_in, jump_out, jump_in, last_out, last_in,
+    r_sem, w_sem, wx, cx, az, ay, fx, xr, fz, sx, xa, hx, ry, rz, rj, lx,
 ):
     depth, row, col = lax.axis_index("depth"), lax.axis_index("row"), lax.axis_index("col")
     z, y, core, x = depth, row // 2, row % 2, col % NX
@@ -50,20 +50,20 @@
 
     half = z // 4
     near_z = [4 * half + (z + k) % 4 for k in (2, 1, 3)]
-    far_z = [4 * (1 - half) + (z + k) % 4 for k in range(4)]
-    z_peers = [*far_z, *near_z]
+    jump = 4 * (1 - half) + z % 4
     y_peers = [(y + k) % NY for k in (2, 1, 3)]
     x_peers = [(x + k) % NX for k in (2, 1, 3)]
     y_order = (y_peers[1], y_peers[2], y_peers[0])
     x_order = (x_peers[1], x_peers[2], x_peers[0])
-    along_z = [at(z=p) for p in z_peers]
+    along_z = [at(z=p) for p in near_z]
+    over = at(z=jump)
     along_y = [at(y=p) for p in y_peers]
     along_x = [at(col=col - x + p) for p in x_peers]
     other = at(core=1 - core)
     far = at(col=(col + NX) % (2 * NX))
 
     barrier = pltpu.get_barrier_semaphore()
-    everyone = [far, *along_z, *along_y, *along_x, other]
+    everyone = [far, over, *along_z, *along_y, *along_x, other]
     for d in everyone:
         pl.semaphore_signal(barrier, inc=1, device_id=d, device_id_type=MESH)
     row_loads = [pltpu.make_async_copy(ref, rows_in.at[i], r_sem.at[i]) for i, ref in enumerate((tok_ref, grad_ref))]
@@ -106,17 +106,28 @@
         def _():
             arrive(mine, cx, ())
 
-        for p, d in zip(z_peers, along_z, strict=True):
+        send(mine, mine, az, (a, jump), (a, z), over)
+        for p, d in zip(near_z, along_z, strict=True):
             send(mine, mine, az, (a, p), (a, z), d)
     for i, ref in enumerate((w_up_ref, w_down_ref)):
         send(ref, weights.at[i, core], wx, (i,), (i,), other)
 
+    def crossed(p):
+        return 4 * (1 - half) + p % 4
+
+    def pass_on(a):
+        block = pieces.at[a, y, jump]
+        arrive(block, az, (a, jump))
+        for p, d in zip(near_z, along_z, strict=True):
+            send(block, block, az, (a, crossed(p)), (a, jump), d)
+
     def part_of(k, q):
         return pieces.at[k // 2, q, pl.ds(4 * (half if k % 2 == 0 else 1 - half), 4)]
 
     def over_y(k):
         a = k // 2
-        for p in near_z if k % 2 == 0 else reversed(far_z):
+        for p in near_z:
+            p = p if k % 2 == 0 else crossed(p)
             arrive(pieces.at[a, y, p], az, (a, p))
         block = part_of(k, y)
         for p, d in zip(y_peers, along_y, strict=True):
@@ -213,11 +224,19 @@
                 for r in range(2)
             ]
             z_out[k, :, parity] = jnp.concatenate(tiles, axis=1).astype(BF16)
-        a = k // 2
-        for p in near_z if k % 2 == 0 else far_z:
-            send(z_out.at[k, p % 4 // 2, p % 2], z_in.at[a, z], rz, (a, p), (a, z), at(z=p))
-        if k % 2 == 0:
-            z_in[a, z] = z_out[k, z % 4 // 2, z % 2]
+        mine = z % 4
+        for p, d in zip(near_z, along_z, strict=True):
+            send(z_out.at[k, p % 4 // 2, p % 2], z_in.at[k, mine], rz, (k, p % 4), (k, mine), d)
+        z_in[k, mine] = z_out[k, mine // 2, mine % 2]
+
+    def half_sum(k):
+        for p in near_z:
+            arrive(z_in.at[k, p % 4], rz, (k, p % 4))
+        return sum(z_in[k, i].astype(F32) for i in range(4))
+
+    def cross(a):
+        jump_out[a] = half_sum(2 * a + 1).astype(BF16)
+        send(jump_out.at[a], jump_in.at[a], rj, (a,), (a,), over)
 
     def unfolded(v):
         low, high = v[:8], v[8:]
@@ -226,9 +245,9 @@
     last_copy = copy(last_out, last_in, lx, (), (), other)
 
     def finish(a, own_ref):
-        for p in (*near_z, *far_z):
-            arrive(z_in.at[a, p], rz, (a, p))
-        total = sum(z_in[a, i].astype(F32) for i in range(NZ))
+        total = half_sum(2 * a)
+        arrive(jump_in.at[a], rj, (a,))
+        total += jump_in[a].astype(F32)
 
         @pl.when(core == a)
         def _():
@@ -245,32 +264,38 @@
             cols = slice(384 * c, 384 * (c + 1))
             ref[:, cols] = (over_tokens(h, full[s, :, :, cols].reshape(256, 384)) * scale).astype(BF16)
 
-    for k in range(4):
-        over_y(k)
+    over_y(0)
+    pass_on(0)
+    over_y(2)
+    pass_on(1)
+    over_y(1)
+    over_y(3)
     project(0)
+    project(2)
+    to_far(0)
     project(1)
-    to_far(0)
-    project(2)
+    to_far(2)
+    project(3)
     to_far(1)
-    project(3)
-    to_far(2)
     to_far(3)
     activate(0)
-    activate(1)
     activate(2)
     back(0)
+    activate(1)
+    back(2)
     activate(3)
     back(1)
-    back(2)
     to_z(0)
     back(3)
+    to_z(2)
     to_z(1)
-    to_z(2)
-    to_z(3)
     for k in range(4):
         arrive(full.at[1 - core, k], fx, (k,))
         arrive(hidden.at[1 - core, k, :, core], hx, (k,))
     weight_grad(0, gwu_ref)
+    to_z(3)
+    cross(0)
+    cross(1)
     weight_grad(1, gwd_ref)
     finish(0, out_ref)
     finish(1, gin_ref)
@@ -332,12 +357,14 @@
             pltpu.VMEM((4, NY, 16, 1536), BF16),
             pltpu.VMEM((4, NY, 16, 1536), BF16),
             pltpu.VMEM((4, 2, 2, 16, 384), BF16),
-            pltpu.VMEM((2, NZ, 16, 384), BF16),
+            pltpu.VMEM((4, 4, 16, 384), BF16),
+            pltpu.VMEM((2, 16, 384), BF16),
+            pltpu.VMEM((2, 16, 384), BF16),
             pltpu.VMEM((16, 384), BF16),
             pltpu.VMEM((16, 384), BF16),
             dma((2,)), dma((2,)), dma((2, 2)), dma((2,)),
             dma((2, 2, NZ)), dma((2, 4, NY)), dma((2, 4)), dma((2, 4, NX)), dma((2, 4)), dma((2, 4)), dma((2, 4, NX)),
-            dma((2, 4)), dma((2, 4, NY)), dma((2, 2, NZ)), dma((2,)),
+            dma((2, 4)), dma((2, 4, NY)), dma((2, 4, 4)), dma((2, 2)), dma((2,)),
         ],
         compiler_params=pltpu.CompilerParams(
             collective_id=0, has_side_effects=True, vmem_limit_bytes=48 << 20

time: 70.4 us -> 69.1 us (0.982)
  Pallas kernels: 69.6 us -> 68.2 us
    pallas_call x1, Pallas kernels: 68.1 us -> 66.8 us  [local(): pl.pallas_call(functools.partial(kernel, scale), name='ffn', out_shape=tu...]
where the time goes in v4:
time: 69.1 us; the launch traced here: 68.9 us
  Pallas kernels  68.2 us (99%)
    pallas_call x1, Pallas kernels, local(): pl.pallas_call(functools.partial(kernel, scale), name='ffn', out_shape=tu...  66.8 us
    pallas_call x1, Pallas kernels, local(): pl.pallas_call(write_out, name='write_out', out_shape=tuple((pltpu.HBM(a....  1.45 us

profile of v4, /device:TPU:1, one launch (start us, length us, event | category | flops | bytes accessed | tf_op | source)
XLA Modules:
  0.0 68.9 jit_solution(12766900398069803549)
XLA Ops:
  0.6 66.8 %ffn.1 = (bf16[4,1536]{1,0:T(4,128)(2,1)S(1)}, bf16[4,1536]{1,0:T(4,128)(2,1)S(1)}, bf16[384,1536]{1,0:T(8,128)(2,1)S(1)}, bf16[384,1536]{1,0:T(8,128)(2,1)S(1)}) custom-call(bf16[4,1536]{1,0:T(4,128)(2,1)} %tok_ref.1, bf16[384,1536]{1,0:T(8,128)(2,1)} %w_up_ref.1, bf16[384,1536]{1,0:T(8,128)(2,1)} %w_down_ref.1, bf16[4,1536]{1,0:T(4,128)(2,1)} %grad_ref.1), custom_call_target="tpu_custom_call" | custom-call | tf_op jit(solution)/shard_map/ffn/pallas_call | solution.py:338
  67.4 1.4 %write_out.1 = (bf16[4,1536]{1,0:T(4,128)(2,1)}, bf16[4,1536]{1,0:T(4,128)(2,1)}, bf16[384,1536]{1,0:T(8,128)(2,1)}, bf16[384,1536]{1,0:T(8,128)(2,1)}) custom-call(bf16[4,1536]{1,0:T(4,128)(2,1)S(1)} %get-tuple-element.8.refs_0_, bf16[4,1536]{1,0:T(4,128)(2,1)S(1)} %get-tuple-element.9.refs_1_, bf16[384,1536]{1,0:T(8,128)(2,1)S(1)} %get-tuple-element.10.refs_2_, ...), custom_call_target="tpu_custom_call" | custom-call | tf_op jit(solution)/shard_map/write_out/pallas_call | solution.py:373

commit v5 on v4

--- a/solution.py
+++ b/solution.py
@@ -146,20 +146,27 @@
                 block = jnp.where(top, pltpu.roll(first, 4, 1), second)
             full[core, k, rows, 384 * c : 384 * (c + 1)] = block.reshape(16, 384).astype(BF16)
 
-    def project(k):
-        order(k, y)
-        for p in y_order:
-            arrive(part_of(k, p), ay, (k, p))
-            order(k, p)
-        if k == 0:
+    def project(h):
+        pair = (h, 2 + h)
+        for k in pair:
+            order(k, y)
+            for p in y_order:
+                arrive(part_of(k, p), ay, (k, p))
+                order(k, p)
+        if h == 0:
             for i in range(2):
                 loads[i].wait()
                 arrive(weights.at[i, 1 - core], wx, (i,))
+        rows = jnp.concatenate([full[core, k] for k in pair], axis=0)
         for f in range(2):
-            part[k, :, f] = along_rows(full[core, k], weights[core, f]).astype(BF16).reshape(NX, 16, 384)
-        for p, d in zip(x_peers, along_x, strict=True):
-            send(part.at[k, p], xin.at[k, x], xr, (k, p), (k, x), d)
-        send(full.at[core, k], full.at[core, k], fx, (k,), (k,), other)
+            sums = along_rows(rows, weights[core, f]).astype(BF16).reshape(2, NX, 16, 384)
+            for n, k in enumerate(pair):
+                part[k, :, f] = sums[n]
+        for k in pair:
+            for p, d in zip(x_peers, along_x, strict=True):
+                send(part.at[k, p], xin.at[k, x], xr, (k, p), (k, x), d)
+        for k in pair:
+            send(full.at[core, k], full.at[core, k], fx, (k,), (k,), other)
 
     def to_far(a):
         total = part[a, x].astype(F32)
@@ -271,11 +278,9 @@
     over_y(1)
     over_y(3)
     project(0)
-    project(2)
+    project(1)
     to_far(0)
-    project(1)
     to_far(2)
-    project(3)
     to_far(1)
     to_far(3)
     activate(0)

time: 69.1 us -> 70.7 us (1.023)
  Pallas kernels: 68.2 us -> 69.9 us
    pallas_call x1, Pallas kernels: 66.8 us -> 68.4 us  [local(): pl.pallas_call(functools.partial(kernel, scale), name='ffn', out_shape=tu...]
where the time goes in v5:
time: 70.7 us; the launch traced here: 70.5 us
  Pallas kernels  69.9 us (99%)
    pallas_call x1, Pallas kernels, local(): pl.pallas_call(functools.partial(kernel, scale), name='ffn', out_shape=tu...  68.4 us
    pallas_call x1, Pallas kernels, local(): pl.pallas_call(write_out, name='write_out', out_shape=tuple((pltpu.HBM(a....  1.45 us

profile of v5, /device:TPU:1, one launch (start us, length us, event | category | flops | bytes accessed | tf_op | source)
XLA Modules:
  0.0 70.5 jit_solution(11123629748785890780)
XLA Ops:
  0.6 68.4 %ffn.1 = (bf16[4,1536]{1,0:T(4,128)(2,1)S(1)}, bf16[4,1536]{1,0:T(4,128)(2,1)S(1)}, bf16[384,1536]{1,0:T(8,128)(2,1)S(1)}, bf16[384,1536]{1,0:T(8,128)(2,1)S(1)}) custom-call(bf16[4,1536]{1,0:T(4,128)(2,1)} %tok_ref.1, bf16[384,1536]{1,0:T(8,128)(2,1)} %w_up_ref.1, bf16[384,1536]{1,0:T(8,128)(2,1)} %w_down_ref.1, bf16[4,1536]{1,0:T(4,128)(2,1)} %grad_ref.1), custom_call_target="tpu_custom_call" | custom-call | tf_op jit(solution)/shard_map/ffn/pallas_call | solution.py:343
  69.1 1.4 %write_out.1 = (bf16[4,1536]{1,0:T(4,128)(2,1)}, bf16[4,1536]{1,0:T(4,128)(2,1)}, bf16[384,1536]{1,0:T(8,128)(2,1)}, bf16[384,1536]{1,0:T(8,128)(2,1)}) custom-call(bf16[4,1536]{1,0:T(4,128)(2,1)S(1)} %get-tuple-element.8.refs_0_, bf16[4,1536]{1,0:T(4,128)(2,1)S(1)} %get-tuple-element.9.refs_1_, bf16[384,1536]{1,0:T(8,128)(2,1)S(1)} %get-tuple-element.10.refs_2_, ...), custom_call_target="tpu_custom_call" | custom-call | tf_op jit(solution)/shard_map/write_out/pallas_call | solution.py:378
